TPU v7x, 32 devices: a whole 2x2x4 slice. The times are simulated.
32 devices in a mesh: batch: 16 (over z, y, core), coef: 2 (over x).
Axes of the slice: x: 2, y: 2, z: 4, core: 2. Of those that a mesh axis runs over, the one named last changes fastest.
Arguments:
- jac_blocks: bfloat16 [128, 2, 2, 128, 128], P(('batch', 'coef')), may hold values from -0.52734375 to 0.52734375
- col_blocks: int32 [2, 128, 2], P('coef', 'batch'), may hold values from 0 to 15, all different within a row; in each aligned block of 8 rows (0 to 7, 8 to 15, ..., all dimensions but the last counted through in order) at most 2 rows name the same one
- residual: float32 [128, 128], P('batch'), may hold values from -6 to 6
- run_of_half: int32 [256], P('batch'), may hold values from 0 to 255, each once
- run_scale: bfloat16 [256], replicated, may hold values from 0.25 to 4
Outputs:
- diag_blocks: float32 [2, 16, 128, 128], P('coef', 'batch')
- gradient: float32 [2, 16, 128], P('coef', 'batch')
Inputs may be any that keep to these rules, and one draw needn't show every extreme that they name: `col_blocks`: the 2 column blocks of one row block in one group differ. For each group, among the row blocks of one batch index (aligned blocks of the row-block dimension), no column block is named more than 2 times, a bound that some block reaches. `run_of_half`: every run appears exactly once.
All inputs are finite; a program needn't handle non-finite values.
Results may differ from a plain program's by a relative error of at most 0.00043.
Values may be sent and summed in bfloat16 or wider, within the bound.
A program may use at most 64 MiB of HBM per device.

v0:
```python
import functools

import jax
import jax.numpy as jnp
from jax import lax
from jax.experimental import pallas as pl
from jax.experimental.pallas import tpu as pltpu
from jax.sharding import PartitionSpec as P

BS = 128
HALF = BS // 2
PAIR = 2
ROWS = BS + 8
STEPS = 32766.0
MESH = pl.DeviceIdType.MESH


def kernel(
    n_batch, n_coef, r_dev,
    jac, targets_in, residual_in, runs_in, scale_in, result,
    items, prods, weights, firsts, seconds, targets, residual, runs, scale,
    from_twin, to_twin, packed, sides, got_packed, got_sides,
    own_sem, small_sem, jac_send, jac_recv, twin_sem, hop_sem, side_sem,
):
    b, c = lax.axis_index("batch"), lax.axis_index("coef")
    n_line = n_batch // 4
    core, side, line = lax.rem(b, 2), lax.rem(lax.div(b, 2), 2), lax.div(b, 4)
    twin = b + 1 - 2 * core
    across_b = b + 2 - 4 * side

    def owner(t, s, k):
        return 4 * t + 2 * s + k

    others = [j + lax.div(j + n_line - line, n_line) for j in range(n_line - 1)]

    rows = r_dev * n_coef
    n_items = rows * PAIR

    small = [
        pltpu.make_async_copy(source, target, small_sem.at[i])
        for i, (source, target) in enumerate(
            ((runs_in, runs), (scale_in, scale), (targets_in, targets), (residual_in, residual))
        )
    ]
    for copy in small:
        copy.start()
    own = pltpu.make_async_copy(jac.at[:, c], items.at[c], own_sem)
    own.start()

    barrier = pltpu.get_barrier_semaphore()
    for k in range(1, n_coef):
        pl.semaphore_signal(barrier, inc=1, device_id=(b, lax.rem(c + k, n_coef)), device_id_type=MESH)
    for peer in [twin, across_b] + [owner(t, side, core) for t in others]:
        pl.semaphore_signal(barrier, inc=1, device_id=(peer, c), device_id_type=MESH)
    pl.semaphore_wait(barrier, n_coef + n_line)

    def jac_copy(k, r):
        peer = lax.rem(c + k, n_coef)
        return pltpu.make_async_remote_copy(
            src_ref=jac.at[r, peer], dst_ref=items.at[c, r],
            send_sem=jac_send.at[k, r], recv_sem=jac_recv.at[k, r],
            device_id=(b, peer), device_id_type=MESH,
        )

    def jac_arrival(k, r):
        source = lax.rem(c + n_coef - k, n_coef)
        return pltpu.make_async_remote_copy(
            src_ref=jac.at[r, source], dst_ref=items.at[source, r],
            send_sem=jac_send.at[k, r], recv_sem=jac_recv.at[k, r],
            device_id=(b, source), device_id_type=MESH,
        )

    for k in range(1, n_coef):
        for r in range(r_dev):
            jac_copy(k, r).start()

    for copy in small:
        copy.wait()
    n_runs = scale.shape[0]
    halves = 2 * rows
    along = jnp.broadcast_to(runs[...].astype(jnp.float32), (halves, halves))
    across = lax.broadcasted_iota(jnp.int32, (halves, halves), 0)
    beside = lax.broadcasted_iota(jnp.int32, (halves, halves), 1)
    run = jnp.sum(jnp.where(across == beside, along, 0.0), axis=1, keepdims=True).astype(jnp.int32)
    hot = lax.broadcasted_iota(jnp.int32, (halves, n_runs), 1) == run
    table = jnp.broadcast_to(scale[...].astype(jnp.float32).reshape(1, n_runs), (halves, n_runs))
    picked = jnp.sum(jnp.where(hot, table, 0.0), axis=1, keepdims=True)
    weights[...] = jnp.broadcast_to(picked, (halves, BS))

    prods[n_items] = jnp.zeros((ROWS, BS), jnp.float32)

    def find(l, _):
        first, second = jnp.int32(n_items), jnp.int32(n_items)
        for i in range(n_items):
            hit = targets[i % PAIR, i // PAIR] == l
            second = jnp.where(hit, first, second)
            first = jnp.where(hit, i, first)
        firsts[l] = first
        seconds[l] = second
        return 0

    lax.fori_loop(0, n_batch, find, 0)

    lane = lax.broadcasted_iota(jnp.int32, (1, BS), 1)
    sub = lax.broadcasted_iota(jnp.int32, (16, BS), 0)

    def multiply(source, r):
        row = source * r_dev + r
        top = weights[pl.ds(2 * row, 1), :]
        low = weights[pl.ds(2 * row + 1, 1), :]
        scaled = jnp.where(lane < HALF, top, low) * residual[pl.ds(row, 1), :]
        part0 = scaled.astype(jnp.bfloat16).astype(jnp.float32)
        part1 = (scaled - part0).astype(jnp.bfloat16).astype(jnp.float32)
        part2 = scaled - part0 - part1
        parts = jnp.where(sub == 0, part0, jnp.where(sub == 1, part1, jnp.where(sub == 2, part2, 0.0)))
        parts = parts.astype(jnp.bfloat16)
        both = jnp.concatenate([items[source, r, s] for s in range(PAIR)], axis=1)
        terms = jnp.dot(parts, both, preferred_element_type=jnp.float32)
        terms = terms[0:8] + terms[8:16]
        for s in range(PAIR):
            block = items[source, r, s]
            wide = block.astype(jnp.float32)
            weighted = jnp.concatenate([wide[:HALF] * top, wide[HALF:] * low], axis=0).astype(jnp.bfloat16)
            slot = row * PAIR + s
            prods[slot, 0:BS, :] = lax.dot_general(
                block, weighted, (((0,), (0,)), ((), ())), preferred_element_type=jnp.float32
            )
            prods[slot, BS:ROWS, :] = terms[:, s * BS:(s + 1) * BS]

    own.wait()
    for r in range(r_dev):
        multiply(c, r)
    for k in range(1, n_coef):
        for r in range(r_dev):
            jac_arrival(k, r).wait_recv()
            multiply(lax.rem(c + n_coef - k, n_coef), r)

    def partial(l):
        return prods[firsts[l]] + prods[seconds[l]]

    def send(src, dst, i, j, sems, peer):
        return pltpu.make_async_remote_copy(
            src_ref=src.at[i], dst_ref=dst.at[j], send_sem=sems[0].at[i], recv_sem=sems[1].at[j],
            device_id=(peer, c), device_id_type=MESH,
        )

    def twin_copy(h, d):
        return send(to_twin.at[h], from_twin.at[h], d, d, (twin_sem.at[0, h], twin_sem.at[1, h]), twin)

    for h in (0, 1):
        for t in range(n_line):
            s = 1 - side if h == 0 else side
            to_twin[h, t] = partial(owner(t, s, 1 - core))
            twin_copy(h, t).start()

    sub8 = lax.broadcasted_iota(jnp.int32, (8, BS), 0)

    def hop_copies(h, i):
        peer = across_b if h == 0 else owner(i, side, core)
        j = i if h == 0 else line
        return (
            send(sides.at[h], got_sides.at[h], i, j, (side_sem.at[0, h], side_sem.at[1, h]), peer),
            send(packed.at[h], got_packed.at[h], i, j, (hop_sem.at[0, h], hop_sem.at[1, h]), peer),
        )

    def arrivals(h, j):
        peer = across_b if h == 0 else owner(j, side, core)
        return (
            send(sides.at[h], got_sides.at[h], j, j, (side_sem.at[0, h], side_sem.at[1, h]), peer),
            send(packed.at[h], got_packed.at[h], j, j, (hop_sem.at[0, h], hop_sem.at[1, h]), peer),
        )

    def pack(h, d, total):
        block = total[0:BS]
        largest = jnp.maximum(jnp.max(jnp.abs(block), axis=0, keepdims=True), 2e-34)
        packed[h, d] = jnp.round(block * (STEPS / largest)).astype(jnp.int32).astype(jnp.int16)
        grad = jnp.sum(total[BS:ROWS], axis=0, keepdims=True)
        sides[h, d] = jnp.where(sub8 == 0, grad, jnp.broadcast_to(largest * (1.0 / STEPS), (8, BS)))
        for copy in hop_copies(h, d):
            copy.start()

    def unpack(h, d):
        for copy in arrivals(h, d):
            copy.wait_recv()
        aside = got_sides[h, d]
        block = got_packed[h, d].astype(jnp.int32).astype(jnp.float32) * aside[1:2]
        return jnp.concatenate([block, jnp.where(sub8 == 0, aside, 0.0)], axis=0)

    for t in range(n_line):
        twin_copy(0, t).wait_recv()
        pack(0, t, partial(owner(t, 1 - side, core)) + from_twin[0, t])

    for t in others + [line]:
        twin_copy(1, t).wait_recv()
        total = partial(owner(t, side, core)) + from_twin[1, t]
        total = total + unpack(0, t)
        if t is not line:
            pack(1, t, total)
    for t in others:
        total = total + unpack(1, t)
    result[0:BS] = total[0:BS]
    result[BS:ROWS] = jnp.broadcast_to(jnp.sum(total[BS:ROWS], axis=0, keepdims=True), (8, BS))

    for k in range(1, n_coef):
        for r in range(r_dev):
            jac_copy(k, r).wait_send()
    for h in (0, 1):
        for t in range(n_line):
            twin_copy(h, t).wait_send()
        for t in range(n_line) if h == 0 else others:
            for copy in hop_copies(h, t):
                copy.wait_send()


def write(result, diag, gradient, sem):
    copies = (
        pltpu.make_async_copy(result.at[0:BS], diag.at[0, 0], sem.at[0]),
        pltpu.make_async_copy(result.at[BS:BS + 1], gradient.at[0], sem.at[1]),
    )
    for copy in copies:
        copy.start()
    for copy in copies:
        copy.wait()


def shards(jac_blocks, col_blocks, residual, run_of_half, run_scale):
    n_batch, n_coef = lax.axis_size("batch"), lax.axis_size("coef")
    r_dev = jac_blocks.shape[0]
    rows = r_dev * n_coef
    n_items = rows * PAIR
    n_line = n_batch // 4
    vmem = pl.BlockSpec(memory_space=pltpu.VMEM)
    hbm = pl.BlockSpec(memory_space=pltpu.HBM)
    result = pl.pallas_call(
        functools.partial(kernel, n_batch, n_coef, r_dev),
        out_shape=pltpu.VMEM((ROWS, BS), jnp.float32),
        in_specs=[hbm] * 5,
        out_specs=vmem,
        scratch_shapes=[
            pltpu.VMEM((n_coef, r_dev, PAIR, BS, BS), jnp.bfloat16),
            pltpu.VMEM((n_items + 1, ROWS, BS), jnp.float32),
            pltpu.VMEM((2 * rows, BS), jnp.float32),
            pltpu.SMEM((n_batch,), jnp.int32),
            pltpu.SMEM((n_batch,), jnp.int32),
            pltpu.SMEM((PAIR, rows), jnp.int32),
            pltpu.VMEM((rows, BS), jnp.float32),
            pltpu.VMEM((1, 2 * rows), jnp.int32),
            pltpu.VMEM(run_scale.shape, run_scale.dtype),
            pltpu.VMEM((2, n_line, ROWS, BS), jnp.float32),
            pltpu.VMEM((2, n_line, ROWS, BS), jnp.float32),
            pltpu.VMEM((2, n_line, BS, BS), jnp.int16),
            pltpu.VMEM((2, n_line, 8, BS), jnp.float32),
            pltpu.VMEM((2, n_line, BS, BS), jnp.int16),
            pltpu.VMEM((2, n_line, 8, BS), jnp.float32),
            pltpu.SemaphoreType.DMA,
            pltpu.SemaphoreType.DMA((4,)),
            pltpu.SemaphoreType.DMA((n_coef, r_dev)),
            pltpu.SemaphoreType.DMA((n_coef, r_dev)),
            pltpu.SemaphoreType.DMA((2, 2, n_line)),
            pltpu.SemaphoreType.DMA((2, 2, n_line)),
            pltpu.SemaphoreType.DMA((2, 2, n_line)),
        ],
        compiler_params=pltpu.CompilerParams(
            collective_id=0, has_side_effects=True, vmem_limit_bytes=60 * 1024 * 1024
        ),
    )(
        jac_blocks,
        col_blocks[0].T,
        residual,
        run_of_half.reshape(1, -1),
        run_scale,
    )
    return pl.pallas_call(
        write,
        out_shape=(
            jax.ShapeDtypeStruct((1, 1, BS, BS), jnp.float32),
            jax.ShapeDtypeStruct((1, 1, BS), jnp.float32),
        ),
        in_specs=[vmem],
        out_specs=(hbm, hbm),
        scratch_shapes=[pltpu.SemaphoreType.DMA((2,))],
        compiler_params=pltpu.CompilerParams(vmem_limit_bytes=1024 * 1024),
    )(result)


def solution(mesh):
    in_specs = (
        P(("batch", "coef"), None, None, None, None),
        P("coef", "batch", None),
        P("batch", None),
        P("batch"),
        P(),
    )
    out_specs = (P("coef", "batch", None, None), P("coef", "batch", None))
    return jax.shard_map(shards, mesh=mesh, in_specs=in_specs, out_specs=out_specs, check_vma=False)
```

profile of v0, /device:TPU:0, one launch (start us, length us, event | category | flops | bytes accessed | tf_op | source)
XLA Modules:
  0.0 22.9 jit_solution(4976911656570586280)
XLA Ops:
  0.6 21.6 %shard_map.68.result = f32[136,128]{1,0:T(8,128)S(1)} custom-call(bf16[4,2,2,128,128]{4,3,2,1,0:T(8,128)(2,1)} %jac.1, s32[2,8]{1,0:T(2,128)} %bitcast.4, f32[8,128]{1,0:T(8,128)} %residual_in.1, s32[1,16]{1,0:T(1,128)} %bitcast.5, bf16[256]{0:T(256)(128)(2,1)} %scale_in.1), custom_call_target="tpu_custom_call" | custom-call | tf_op jit(solution)/shard_map/pallas_call | solution.py:234
  22.3 0.7 %shard_map.69 = (f32[1,1,128,128]{3,2,1,0:T(8,128)}, f32[1,1,128]{2,1,0:T(1,128)}) custom-call(f32[136,128]{1,0:T(8,128)S(1)} %shard_map.68.result), custom_call_target="tpu_custom_call" | custom-call | tf_op jit(solution)/shard_map/pallas_call | solution.py:273
where the time goes:
time: 23.2 us; the launch traced here: 22.9 us
  Pallas kernels  22.3 us (96%)
  between operations  0.64 us (3%)
    pallas_call x1, Pallas kernels, shards(): pl.pallas_call(functools.partial(kernel, n_batch, n_coef, r_dev), out_sha...  21.6 us
    pallas_call x1, Pallas kernels, shards(): pl.pallas_call(write, out_shape=(jax.ShapeDtypeStruct((1, 1, BS, BS), jnp...  0.65 us

commit v1 on v0

--- a/solution.py
+++ b/solution.py
@@ -23,15 +23,11 @@
     own_sem, small_sem, jac_send, jac_recv, twin_sem, hop_sem, side_sem,
 ):
     b, c = lax.axis_index("batch"), lax.axis_index("coef")
-    n_line = n_batch // 4
-    core, side, line = lax.rem(b, 2), lax.rem(lax.div(b, 2), 2), lax.div(b, 4)
+    chips = n_batch // 2
+    core, chip = lax.rem(b, 2), lax.div(b, 2)
     twin = b + 1 - 2 * core
-    across_b = b + 2 - 4 * side
-
-    def owner(t, s, k):
-        return 4 * t + 2 * s + k
-
-    others = [j + lax.div(j + n_line - line, n_line) for j in range(n_line - 1)]
+
+    others = [j + lax.div(j + chips - chip, chips) for j in range(chips - 1)]
 
     rows = r_dev * n_coef
     n_items = rows * PAIR
@@ -50,9 +46,9 @@
     barrier = pltpu.get_barrier_semaphore()
     for k in range(1, n_coef):
         pl.semaphore_signal(barrier, inc=1, device_id=(b, lax.rem(c + k, n_coef)), device_id_type=MESH)
-    for peer in [twin, across_b] + [owner(t, side, core) for t in others]:
+    for peer in [twin] + [2 * t + core for t in others]:
         pl.semaphore_signal(barrier, inc=1, device_id=(peer, c), device_id_type=MESH)
-    pl.semaphore_wait(barrier, n_coef + n_line)
+    pl.semaphore_wait(barrier, n_coef + chips - 1)
 
     def jac_copy(k, r):
         peer = lax.rem(c + k, n_coef)
@@ -144,72 +140,51 @@
             device_id=(peer, c), device_id_type=MESH,
         )
 
-    def twin_copy(h, d):
-        return send(to_twin.at[h], from_twin.at[h], d, d, (twin_sem.at[0, h], twin_sem.at[1, h]), twin)
-
-    for h in (0, 1):
-        for t in range(n_line):
-            s = 1 - side if h == 0 else side
-            to_twin[h, t] = partial(owner(t, s, 1 - core))
-            twin_copy(h, t).start()
+    def twin_copy(t):
+        return send(to_twin, from_twin, t, t, (twin_sem.at[0], twin_sem.at[1]), twin)
+
+    for t in range(chips):
+        to_twin[t] = partial(2 * t + 1 - core)
+        twin_copy(t).start()
 
     sub8 = lax.broadcasted_iota(jnp.int32, (8, BS), 0)
 
-    def hop_copies(h, i):
-        peer = across_b if h == 0 else owner(i, side, core)
-        j = i if h == 0 else line
+    def copies(i, j, peer):
         return (
-            send(sides.at[h], got_sides.at[h], i, j, (side_sem.at[0, h], side_sem.at[1, h]), peer),
-            send(packed.at[h], got_packed.at[h], i, j, (hop_sem.at[0, h], hop_sem.at[1, h]), peer),
-        )
-
-    def arrivals(h, j):
-        peer = across_b if h == 0 else owner(j, side, core)
-        return (
-            send(sides.at[h], got_sides.at[h], j, j, (side_sem.at[0, h], side_sem.at[1, h]), peer),
-            send(packed.at[h], got_packed.at[h], j, j, (hop_sem.at[0, h], hop_sem.at[1, h]), peer),
-        )
-
-    def pack(h, d, total):
+            send(packed, got_packed, i, j, (hop_sem.at[0], hop_sem.at[1]), peer),
+            send(sides, got_sides, i, j, (side_sem.at[0], side_sem.at[1]), peer),
+        )
+
+    for t in others:
+        twin_copy(t).wait_recv()
+        total = partial(2 * t + core) + from_twin[t]
         block = total[0:BS]
         largest = jnp.maximum(jnp.max(jnp.abs(block), axis=0, keepdims=True), 2e-34)
-        packed[h, d] = jnp.round(block * (STEPS / largest)).astype(jnp.int32).astype(jnp.int16)
+        packed[t] = jnp.round(block * (STEPS / largest)).astype(jnp.int32).astype(jnp.int16)
         grad = jnp.sum(total[BS:ROWS], axis=0, keepdims=True)
-        sides[h, d] = jnp.where(sub8 == 0, grad, jnp.broadcast_to(largest * (1.0 / STEPS), (8, BS)))
-        for copy in hop_copies(h, d):
+        sides[t] = jnp.where(sub8 == 0, grad, jnp.broadcast_to(largest * (1.0 / STEPS), (8, BS)))
+        for copy in copies(t, chip, 2 * t + core):
             copy.start()
 
-    def unpack(h, d):
-        for copy in arrivals(h, d):
+    twin_copy(chip).wait_recv()
+    total = partial(b) + from_twin[chip]
+    for t in others:
+        for copy in copies(t, t, 2 * t + core):
             copy.wait_recv()
-        aside = got_sides[h, d]
-        block = got_packed[h, d].astype(jnp.int32).astype(jnp.float32) * aside[1:2]
-        return jnp.concatenate([block, jnp.where(sub8 == 0, aside, 0.0)], axis=0)
-
-    for t in range(n_line):
-        twin_copy(0, t).wait_recv()
-        pack(0, t, partial(owner(t, 1 - side, core)) + from_twin[0, t])
-
-    for t in others + [line]:
-        twin_copy(1, t).wait_recv()
-        total = partial(owner(t, side, core)) + from_twin[1, t]
-        total = total + unpack(0, t)
-        if t is not line:
-            pack(1, t, total)
-    for t in others:
-        total = total + unpack(1, t)
+        aside = got_sides[t]
+        block = got_packed[t].astype(jnp.int32).astype(jnp.float32) * aside[1:2]
+        total = total + jnp.concatenate([block, jnp.where(sub8 == 0, aside, 0.0)], axis=0)
     result[0:BS] = total[0:BS]
     result[BS:ROWS] = jnp.broadcast_to(jnp.sum(total[BS:ROWS], axis=0, keepdims=True), (8, BS))
 
     for k in range(1, n_coef):
         for r in range(r_dev):
             jac_copy(k, r).wait_send()
-    for h in (0, 1):
-        for t in range(n_line):
-            twin_copy(h, t).wait_send()
-        for t in range(n_line) if h == 0 else others:
-            for copy in hop_copies(h, t):
-                copy.wait_send()
+    for t in range(chips):
+        twin_copy(t).wait_send()
+    for t in others:
+        for copy in copies(t, chip, 2 * t + core):
+            copy.wait_send()
 
 
 def write(result, diag, gradient, sem):
@@ -228,7 +203,7 @@
     r_dev = jac_blocks.shape[0]
     rows = r_dev * n_coef
     n_items = rows * PAIR
-    n_line = n_batch // 4
+    chips = n_batch // 2
     vmem = pl.BlockSpec(memory_space=pltpu.VMEM)
     hbm = pl.BlockSpec(memory_space=pltpu.HBM)
     result = pl.pallas_call(
@@ -246,19 +221,19 @@
             pltpu.VMEM((rows, BS), jnp.float32),
             pltpu.VMEM((1, 2 * rows), jnp.int32),
             pltpu.VMEM(run_scale.shape, run_scale.dtype),
-            pltpu.VMEM((2, n_line, ROWS, BS), jnp.float32),
-            pltpu.VMEM((2, n_line, ROWS, BS), jnp.float32),
-            pltpu.VMEM((2, n_line, BS, BS), jnp.int16),
-            pltpu.VMEM((2, n_line, 8, BS), jnp.float32),
-            pltpu.VMEM((2, n_line, BS, BS), jnp.int16),
-            pltpu.VMEM((2, n_line, 8, BS), jnp.float32),
+            pltpu.VMEM((chips, ROWS, BS), jnp.float32),
+            pltpu.VMEM((chips, ROWS, BS), jnp.float32),
+            pltpu.VMEM((chips, BS, BS), jnp.int16),
+            pltpu.VMEM((chips, 8, BS), jnp.float32),
+            pltpu.VMEM((chips, BS, BS), jnp.int16),
+            pltpu.VMEM((chips, 8, BS), jnp.float32),
             pltpu.SemaphoreType.DMA,
             pltpu.SemaphoreType.DMA((4,)),
             pltpu.SemaphoreType.DMA((n_coef, r_dev)),
             pltpu.SemaphoreType.DMA((n_coef, r_dev)),
-            pltpu.SemaphoreType.DMA((2, 2, n_line)),
-            pltpu.SemaphoreType.DMA((2, 2, n_line)),
-            pltpu.SemaphoreType.DMA((2, 2, n_line)),
+            pltpu.SemaphoreType.DMA((2, chips)),
+            pltpu.SemaphoreType.DMA((2, chips)),
+            pltpu.SemaphoreType.DMA((2, chips)),
         ],
         compiler_params=pltpu.CompilerParams(
             collective_id=0, has_side_effects=True, vmem_limit_bytes=60 * 1024 * 1024

time: 23.2 us -> 22.4 us (0.966)
  Pallas kernels: 22.3 us -> 21.5 us
    pallas_call x1, Pallas kernels: 21.6 us -> 20.9 us  [shards(): pl.pallas_call(functools.partial(kernel, n_batch, n_coef, r_dev), out_sha...]
where the time goes in v1:
time: 22.4 us; the launch traced here: 22.2 us
  Pallas kernels  21.5 us (96%)
  between operations  0.64 us (3%)
    pallas_call x1, Pallas kernels, shards(): pl.pallas_call(functools.partial(kernel, n_batch, n_coef, r_dev), out_sha...  20.9 us
    pallas_call x1, Pallas kernels, shards(): pl.pallas_call(write, out_shape=(jax.ShapeDtypeStruct((1, 1, BS, BS), jnp...  0.65 us

profile of v1, /device:TPU:0, one launch (start us, length us, event | category | flops | bytes accessed | tf_op | source)
XLA Modules:
  0.0 22.2 jit_solution(3760395743093541939)
XLA Ops:
  0.6 20.9 %shard_map.68.result = f32[136,128]{1,0:T(8,128)S(1)} custom-call(bf16[4,2,2,128,128]{4,3,2,1,0:T(8,128)(2,1)} %jac.1, s32[2,8]{1,0:T(2,128)} %bitcast.4, f32[8,128]{1,0:T(8,128)} %residual_in.1, s32[1,16]{1,0:T(1,128)} %bitcast.5, bf16[256]{0:T(256)(128)(2,1)} %scale_in.1), custom_call_target="tpu_custom_call" | custom-call | tf_op jit(solution)/shard_map/pallas_call | solution.py:209
  21.5 0.7 %shard_map.69 = (f32[1,1,128,128]{3,2,1,0:T(8,128)}, f32[1,1,128]{2,1,0:T(1,128)}) custom-call(f32[136,128]{1,0:T(8,128)S(1)} %shard_map.68.result), custom_call_target="tpu_custom_call" | custom-call | tf_op jit(solution)/shard_map/pallas_call | solution.py:248

commit v2 on v1

--- a/solution.py
+++ b/solution.py
@@ -24,10 +24,18 @@
 ):
     b, c = lax.axis_index("batch"), lax.axis_index("coef")
     chips = n_batch // 2
+    n_half = chips // 4
     core, chip = lax.rem(b, 2), lax.div(b, 2)
+    side, line = lax.rem(chip, 2), lax.div(chip, 2)
     twin = b + 1 - 2 * core
-
-    others = [j + lax.div(j + chips - chip, chips) for j in range(chips - 1)]
+    half = lax.div(line, n_half)
+    place = line - half * n_half
+    far = [(1 - half) * n_half + j for j in range(n_half)]
+    near = [half * n_half + j + lax.div(j + n_half - place, n_half) for j in range(n_half - 1)]
+    here = [2 * t + side for t in near] + [2 * t + 1 - side for t in near] + [2 * line + 1 - side]
+    crossing = [2 * t + side for t in far]
+    crossing_pair = [2 * t + 1 - side for t in far]
+    order = crossing_pair + here + crossing + [chip]
 
     rows = r_dev * n_coef
     n_items = rows * PAIR
@@ -46,9 +54,9 @@
     barrier = pltpu.get_barrier_semaphore()
     for k in range(1, n_coef):
         pl.semaphore_signal(barrier, inc=1, device_id=(b, lax.rem(c + k, n_coef)), device_id_type=MESH)
-    for peer in [twin] + [2 * t + core for t in others]:
+    for peer in [twin] + [2 * t + core for t in here + crossing]:
         pl.semaphore_signal(barrier, inc=1, device_id=(peer, c), device_id_type=MESH)
-    pl.semaphore_wait(barrier, n_coef + chips - 1)
+    pl.semaphore_wait(barrier, n_coef + len(here) + len(crossing))
 
     def jac_copy(k, r):
         peer = lax.rem(c + k, n_coef)
@@ -143,7 +151,7 @@
     def twin_copy(t):
         return send(to_twin, from_twin, t, t, (twin_sem.at[0], twin_sem.at[1]), twin)
 
-    for t in range(chips):
+    for t in order:
         to_twin[t] = partial(2 * t + 1 - core)
         twin_copy(t).start()
 
@@ -155,35 +163,53 @@
             send(sides, got_sides, i, j, (side_sem.at[0], side_sem.at[1]), peer),
         )
 
-    for t in others:
+    across_b = b + 2 - 4 * side
+
+    def departures():
+        hops = [copies(2 * t + 1 - side, 2 * t + side, across_b) for t in far]
+        return hops + [copies(t, chip, 2 * t + core) for t in here + crossing]
+
+    def total_of(t):
         twin_copy(t).wait_recv()
-        total = partial(2 * t + core) + from_twin[t]
+        return partial(2 * t + core) + from_twin[t]
+
+    def pack(t, total):
         block = total[0:BS]
         largest = jnp.maximum(jnp.max(jnp.abs(block), axis=0, keepdims=True), 2e-34)
         packed[t] = jnp.round(block * (STEPS / largest)).astype(jnp.int32).astype(jnp.int16)
         grad = jnp.sum(total[BS:ROWS], axis=0, keepdims=True)
         sides[t] = jnp.where(sub8 == 0, grad, jnp.broadcast_to(largest * (1.0 / STEPS), (8, BS)))
-        for copy in copies(t, chip, 2 * t + core):
-            copy.start()
-
-    twin_copy(chip).wait_recv()
-    total = partial(b) + from_twin[chip]
-    for t in others:
+
+    def unpack(t):
         for copy in copies(t, t, 2 * t + core):
             copy.wait_recv()
         aside = got_sides[t]
         block = got_packed[t].astype(jnp.int32).astype(jnp.float32) * aside[1:2]
-        total = total + jnp.concatenate([block, jnp.where(sub8 == 0, aside, 0.0)], axis=0)
+        return jnp.concatenate([block, jnp.where(sub8 == 0, aside, 0.0)], axis=0)
+
+    sent = departures()
+    for i, t in enumerate(crossing_pair + here):
+        pack(t, total_of(t))
+        for copy in sent[i]:
+            copy.start()
+    for i, t in enumerate(crossing):
+        pack(t, total_of(t) + unpack(crossing_pair[i]))
+        for copy in sent[len(far) + len(here) + i]:
+            copy.start()
+
+    total = total_of(chip)
+    for t in here + crossing:
+        total = total + unpack(t)
     result[0:BS] = total[0:BS]
     result[BS:ROWS] = jnp.broadcast_to(jnp.sum(total[BS:ROWS], axis=0, keepdims=True), (8, BS))
 
     for k in range(1, n_coef):
         for r in range(r_dev):
             jac_copy(k, r).wait_send()
-    for t in range(chips):
+    for t in order:
         twin_copy(t).wait_send()
-    for t in others:
-        for copy in copies(t, chip, 2 * t + core):
+    for pair in departures():
+        for copy in pair:
             copy.wait_send()
 
 

time: 22.4 us -> 22.1 us (0.987)
  no operation moved by 1% of the time
where the time goes in v2:
time: 22.1 us; the launch traced here: 21.9 us
  Pallas kernels  21.3 us (96%)
  between operations  0.64 us (3%)
    pallas_call x1, Pallas kernels, shards(): pl.pallas_call(functools.partial(kernel, n_batch, n_coef, r_dev), out_sha...  20.7 us
    pallas_call x1, Pallas kernels, shards(): pl.pallas_call(write, out_shape=(jax.ShapeDtypeStruct((1, 1, BS, BS), jnp...  0.65 us

profile of v2, /device:TPU:0, one launch (start us, length us, event | category | flops | bytes accessed | tf_op | source)
XLA Modules:
  0.0 21.9 jit_solution(485993703301449282)
XLA Ops:
  0.6 20.7 %shard_map.68.result = f32[136,128]{1,0:T(8,128)S(1)} custom-call(bf16[4,2,2,128,128]{4,3,2,1,0:T(8,128)(2,1)} %jac.1, s32[2,8]{1,0:T(2,128)} %bitcast.4, f32[8,128]{1,0:T(8,128)} %residual_in.1, s32[1,16]{1,0:T(1,128)} %bitcast.5, bf16[256]{0:T(256)(128)(2,1)} %scale_in.1), custom_call_target="tpu_custom_call" | custom-call | tf_op jit(solution)/shard_map/pallas_call | solution.py:235
  21.3 0.7 %shard_map.69 = (f32[1,1,128,128]{3,2,1,0:T(8,128)}, f32[1,1,128]{2,1,0:T(1,128)}) custom-call(f32[136,128]{1,0:T(8,128)S(1)} %shard_map.68.result), custom_call_target="tpu_custom_call" | custom-call | tf_op jit(solution)/shard_map/pallas_call | solution.py:274
